TPU v7x, 32 devices: a whole 2x2x4 slice. The times are simulated.
32 devices in a mesh: ctx: 4 (over x, core), tp: 4 (over z), pp: 2 (over y).
Axes of the slice: x: 2, y: 2, z: 4, core: 2. Of those that a mesh axis runs over, the one named last changes fastest.
Arguments:
- queries: bfloat16 [2, 512, 8192], P('pp', 'ctx', 'tp'), may hold values from -6 to 6
- key_feats: bfloat16 [2, 512, 8192], P('pp', 'ctx', 'tp'), may hold values from -6 to 6
- value_feats: bfloat16 [2, 512, 8192], P('pp', 'ctx', 'tp'), may hold values from -6 to 6
- cotangent: bfloat16 [2, 512, 8192], P('pp', 'ctx', 'tp'), may hold values from -70 to 70
- filters: float32 [2, 512, 128], P('pp', 'tp'), may hold values from -0.5 to 0.5
Outputs:
- grad_queries: bfloat16 [2, 512, 8192], P('pp', 'ctx', 'tp')
- grad_keys: bfloat16 [2, 512, 8192], P('pp', 'ctx', 'tp')
- handed: bfloat16 [2, 512, 8192], P('pp', 'ctx', 'tp')
- grad_filters: float32 [2, 512, 128], P('pp', 'tp')
All inputs are finite; a program needn't handle non-finite values.
Results may differ from a plain program's by a relative error of at most 0.0058.
Values may be sent and summed in bfloat16 or wider, within the bound.
A program may use at most 64 MiB of HBM per device.

v0:
```python
import math

import jax
import jax.numpy as jnp
from jax import lax
from jax.sharding import PartitionSpec as P

TAPS = 128
GROUP = 16
GROUPS = 512


BLOCK_ROWS = 64


def from_behind(block, axis, distance):
    devices = range(lax.axis_size(axis))
    route = [(i - distance, i) for i in devices if i - distance in devices]
    return lax.ppermute(block, axis, route)


def build_kernel(taps_rows, row_count):
    groups_here = taps_rows.shape[0]
    padded = jnp.concatenate(
        [taps_rows, jnp.zeros((groups_here, row_count), taps_rows.dtype)], axis=1
    )
    tiled = jnp.tile(padded, (1, row_count))
    span = row_count + TAPS - 1
    return tiled[:, : row_count * span].reshape(groups_here, row_count, span)


def apply_kernel(kernel, window):
    groups_here, row_count, span = kernel.shape
    pieces = window.reshape(span, groups_here, GROUP)
    result = jnp.einsum("gts,sgc->tgc", kernel, pieces, preferred_element_type=jnp.float32)
    return result.reshape(row_count, groups_here * GROUP)


def apply_blocks(kernel, extended, first, count):
    span = BLOCK_ROWS + TAPS - 1
    parts = [
        apply_kernel(
            kernel,
            extended[
                (first + block_index) * BLOCK_ROWS : (first + block_index) * BLOCK_ROWS + span
            ],
        )
        for block_index in range(count)
    ]
    return jnp.concatenate(parts, axis=0)


def per_device(queries, key_feats, value_feats, cotangent, filters):
    query_rows = queries[0]
    key_rows = key_feats[0]
    value_rows = value_feats[0]
    cot_rows = cotangent[0]
    length = query_rows.shape[0]
    channels = query_rows.shape[1]
    halo_len = TAPS - 1
    block_rows = BLOCK_ROWS
    num_blocks = length // block_rows
    span = block_rows + halo_len
    tail_blocks = TAPS // block_rows
    last_start = length - TAPS
    taps_bf = filters[0].astype(jnp.bfloat16)
    groups_here = taps_bf.shape[0]
    kernel_fwd = build_kernel(taps_bf[:, ::-1], block_rows)
    kernel_back = build_kernel(taps_bf, block_rows)
    product = key_rows * value_rows
    weighted = cot_rows * query_rows
    incoming = from_behind(product[length - halo_len :], "ctx", 1)
    front_ext = jnp.concatenate([incoming, product], axis=0)
    mixed_rows = apply_blocks(kernel_fwd, front_ext, 0, num_blocks)
    grad_q = (cot_rows * mixed_rows).astype(jnp.bfloat16)
    zero_rim = jnp.zeros((halo_len, channels), jnp.bfloat16)
    early_ext = jnp.concatenate([weighted, zero_rim], axis=0)
    head_grads = []
    head_values = []
    head_count = num_blocks - tail_blocks
    following = from_behind(weighted[:halo_len], "ctx", -1)
    late_ext = jnp.concatenate([weighted, following], axis=0)
    last_block = apply_blocks(kernel_back, late_ext, 0, tail_blocks)
    tail_grad = (last_block * value_rows).astype(jnp.bfloat16)
    tail_values = (last_block * key_rows).astype(jnp.bfloat16)
    grad_k = jnp.concatenate(head_grads + [tail_grad], axis=0)
    boundary = jnp.concatenate(head_values + [tail_values], axis=0)
    handed = from_behind(boundary, "pp", -1)
    raw_grad = jnp.zeros((groups_here, TAPS), jnp.float32)
    for block_index in range(num_blocks):
        grad_block = weighted[block_index * block_rows : (block_index + 1) * block_rows].reshape(
            block_rows, groups_here, GROUP
        )
        window = front_ext[block_index * block_rows : block_index * block_rows + span].reshape(
            span, groups_here, GROUP
        )
        pairs = jnp.einsum("tgc,sgc->gts", grad_block, window, preferred_element_type=jnp.float32)
        flat = pairs.reshape(groups_here, block_rows * span)
        flat = jnp.concatenate([flat, jnp.zeros((groups_here, block_rows), jnp.float32)], axis=1)
        skewed = flat.reshape(groups_here, block_rows, span + 1).sum(axis=1)
        raw_grad = raw_grad + skewed[:, :TAPS][:, ::-1]
    clip_level = 0.25 * math.sqrt(lax.axis_size("pp") * GROUPS * TAPS)
    summed = lax.psum(raw_grad, "ctx")
    norm_sq = lax.psum(jnp.sum(summed * summed), ("tp", "pp"))
    factor = jnp.minimum(1.0, clip_level / (jnp.sqrt(norm_sq) + 1e-06))
    grad_f = summed * factor
    return (grad_q[None], grad_k[None], handed[None], grad_f[None])


def solution(mesh):
    placed = (
        P("pp", "ctx", "tp"),
        P("pp", "ctx", "tp"),
        P("pp", "ctx", "tp"),
        P("pp", "ctx", "tp"),
        P("pp", "tp", None),
    )
    return jax.shard_map(
        per_device,
        mesh=mesh,
        in_specs=placed,
        out_specs=(
            P("pp", "ctx", "tp"),
            P("pp", "ctx", "tp"),
            P("pp", "ctx", "tp"),
            P("pp", "tp", None),
        ),
        check_vma=False,
    )
```

profile of v0, /device:TPU:0, one launch (start us, length us, event | category | flops | bytes accessed | tf_op | source)
XLA Modules:
  0.0 176.2 jit_solution(528723281138111936)
XLA Ops:
  7.2 0.0 all-reduce.6.cloned.1.call-start
  7.2 1.3 mul.32
  8.6 0.0 copy-start.3
  8.6 1.0 slice_bitcast_fusion.1
  9.5 3.1 %collective-permute-start = (bf16[127,2048]{1,0:T(8,128)(2,1)}, bf16[127,2048]{1,0:T(8,128)(2,1)}, u32[]{:S(2)}, u32[]{:S(2)}) collective-permute-start(bf16[127,2048]{1,0:T(8,128)(2,1)} %slice_bitcast_fusion.1), channel_id=1, source_target_pairs={{0,8},{8,16},{16,24},{1,9},{9,17},{17,25},{2,10},{10,18},{18,26},{... | collective-permute-start | bytes 1560584 | tf_op jit(solution)/shard_map/ppermute | solution.py:19
  12.7 1.3 mul.35
  14.0 0.0 copy-start.1
  14.0 0.9 slice_bitcast_fusion
  14.9 1.3 collective-permute-start.1
  16.2 0.1 copy.65
  16.4 0.1 rev.9
  16.5 1.0 copy.57
  17.5 1.0 copy.59
  18.5 0.7 tile.20
  19.3 1.8 %slice.67 = bf16[128,12224]{0,1:T(8,128)(2,1)} slice(bf16[128,12288]{0,1:T(8,128)(2,1)S(1)} %bitcast.58), slice={[0:128], [0:12224]} | slice | bytes 6258688 | tf_op jit(solution)/shard_map/slice | solution.py:29
  21.1 3.1 %reshape.85 = bf16[128,64,191]{0,2,1:T(8,128)(2,1)S(1)} reshape(bf16[128,12224]{0,1:T(8,128)(2,1)} %slice.67) | data formatting | bytes 6258688 | tf_op jit(solution)/shard_map/reshape | solution.py:29
  24.1 7.6 %copy.50 = bf16[128,64,191]{2,1,0:T(8,128)(2,1)} copy(bf16[128,64,191]{0,2,1:T(8,128)(2,1)S(1)} %reshape.85) | data formatting | bytes 6258688 | tf_op jit(solution)/shard_map/reshape | solution.py:29
  31.7 0.1 copy.64
  31.8 0.8 tile.8
  32.6 1.8 %slice.63 = bf16[128,12224]{0,1:T(8,128)(2,1)} slice(bf16[128,12288]{0,1:T(8,128)(2,1)S(1)} %bitcast.59), slice={[0:128], [0:12224]} | slice | bytes 6258688 | tf_op jit(solution)/shard_map/slice | solution.py:29
  34.4 3.1 %reshape.82 = bf16[128,64,191]{0,2,1:T(8,128)(2,1)S(1)} reshape(bf16[128,12224]{0,1:T(8,128)(2,1)} %slice.63) | data formatting | bytes 6258688 | tf_op jit(solution)/shard_map/reshape | solution.py:29
  37.4 7.7 %copy.43 = bf16[128,64,191]{2,1,0:T(8,128)(2,1)} copy(bf16[128,64,191]{0,2,1:T(8,128)(2,1)S(1)} %reshape.82) | data formatting | bytes 6258688 | tf_op jit(solution)/shard_map/reshape | solution.py:29
  45.1 0.0 collective-permute-done
  45.1 1.7 fusion.4
  46.8 0.5 copy.41
  47.3 4.5 %fusion.10 = f32[128,64,191]{2,1,0:T(8,128)} fusion(bf16[64,128,16]{0,2,1:T(8,128)(2,1)S(1)} %bitcast.75, bf16[191,128,16]{0,2,1:T(8,128)(2,1)S(1)} %bitcast.60), kind=kOutput, calls=%fused_computation.24 | convolution fusion | flops 50069504 | bytes 7303168 | tf_op jit(solution)/shard_map/tgc,sgc->gts/dot_general | solution.py:97
  51.8 9.1 %reshape.96 = f32[128,12224]{1,0:T(8,128)} reshape(f32[128,64,191]{2,1,0:T(8,128)} %fusion.10) | data formatting | bytes 12517376 | tf_op jit(solution)/shard_map/reshape | solution.py:98
  60.9 6.6 %copy.62 = f32[128,12224]{0,1:T(8,128)} copy(f32[128,12224]{1,0:T(8,128)} %reshape.96) | data formatting | bytes 12517376 | tf_op jit(solution)/shard_map/reshape | solution.py:98
  67.5 4.7 %concatenate.47 = f32[128,12288]{0,1:T(8,128)} pad(f32[128,12224]{0,1:T(8,128)} %copy.62, f32[]{:T(128)} %constant.0.clone.1), padding=0_0x0_64 | pad | bytes 12550148 | tf_op jit(solution)/shard_map/concatenate | solution.py:99
  72.2 3.2 %reduce_sum.27 = f32[128,192]{0,1:T(8,128)S(1)} reduce(f32[128,64,192]{0,2,1:T(8,128)} %bitcast.57, f32[]{:T(128)} %constant.0.clone.1), dimensions={1}, to_apply=%region_0.0 | reduce | flops 1548288 | bytes 6389764 | tf_op jit(solution)/shard_map/reduce_sum | solution.py:100
  75.4 0.5 copy.44
  75.9 4.6 %fusion.11 = f32[128,64,191]{2,1,0:T(8,128)} fusion(bf16[64,128,16]{0,2,1:T(8,128)(2,1)S(1)} %bitcast.74, bf16[191,128,16]{0,2,1:T(8,128)(2,1)S(1)} %bitcast.62), kind=kOutput, calls=%fused_computation.25 | convolution fusion | flops 50069504 | bytes 7303168 | tf_op jit(solution)/shard_map/tgc,sgc->gts/dot_general | solution.py:97
  80.5 9.0 %reshape.97 = f32[128,12224]{1,0:T(8,128)} reshape(f32[128,64,191]{2,1,0:T(8,128)} %fusion.11) | data formatting | bytes 12517376 | tf_op jit(solution)/shard_map/reshape | solution.py:98
  89.5 6.6 %copy.63 = f32[128,12224]{0,1:T(8,128)} copy(f32[128,12224]{1,0:T(8,128)} %reshape.97) | data formatting | bytes 12517376 | tf_op jit(solution)/shard_map/reshape | solution.py:98
  96.1 4.8 %concatenate.48 = f32[128,12288]{0,1:T(8,128)} pad(f32[128,12224]{0,1:T(8,128)} %copy.63, f32[]{:T(128)} %constant.0.clone.1), padding=0_0x0_64 | pad | bytes 12550148 | tf_op jit(solution)/shard_map/concatenate | solution.py:99
  100.9 3.2 %reduce_sum.28 = f32[128,192]{0,1:T(8,128)S(1)} reduce(f32[128,64,192]{0,2,1:T(8,128)} %bitcast.56, f32[]{:T(128)} %constant.0.clone.1), dimensions={1}, to_apply=%region_1.0 | reduce | flops 1548288 | bytes 6389764 | tf_op jit(solution)/shard_map/reduce_sum | solution.py:100
  104.1 0.6 add.18
  104.7 0.0 all-reduce.6.cloned.1.call-update
  104.7 0.0 collective-permute-done.1
  104.7 2.2 %fusion.3 = (bf16[191,2048]{1,0:T(8,128)(2,1)S(1)}, bf16[191,2048]{1,0:T(8,128)(2,1)}) fusion(bf16[128,2048]{1,0:T(8,128)(2,1)S(1)} %bitcast.68, bf16[127,2048]{1,0:T(8,128)(2,1)} %collective-permute-done.1), kind=kLoop, calls=%fused_computation.10 | loop fusion | flops 3129344 | bytes 2609152 | tf_op jit(solution)/shard_map/concatenate | solution.py:82
  106.9 1.3 copy.48
  108.3 3.7 %fusion.8 = f32[128,16,64]{2,1,0:T(8,128)S(1)} fusion(bf16[191,128,16]{0,2,1:T(8,128)(2,1)} %bitcast.71, bf16[128,64,191]{2,1,0:T(8,128)(2,1)} %copy.50), kind=kOutput, calls=%fused_computation.22 | convolution fusion | flops 50069504 | bytes 4435968 | tf_op jit(solution)/shard_map/gts,sgc->tgc/dot_general | solution.py:35
  111.9 1.1 copy.55
  113.1 2.2 %copy.51 = bf16[191,2048]{0,1:T(8,128)(2,1)} copy(bf16[191,2048]{1,0:T(8,128)(2,1)} %get-tuple-element.9) | data formatting | bytes 1564672 | tf_op jit(solution)/shard_map/slice | solution.py:44
  115.3 4.8 %fusion.9 = f32[128,16,64]{2,1,0:T(8,128)} fusion(bf16[191,128,16]{0,2,1:T(8,128)(2,1)} %bitcast.70, bf16[128,64,191]{2,1,0:T(8,128)(2,1)} %copy.50), kind=kOutput, calls=%fused_computation.23 | convolution fusion | flops 50069504 | bytes 4435968 | tf_op jit(solution)/shard_map/gts,sgc->tgc/dot_general | solution.py:35
  120.1 2.3 %copy.56 = f32[64,2048]{1,0:T(8,128)} copy(f32[64,2048]{0,1:T(8,128)} %bitcast.66) | data formatting | bytes 1048576 | tf_op jit(solution)/shard_map/reshape | solution.py:36
  122.4 2.3 %fusion.2 = bf16[128,2048]{1,0:T(8,128)(2,1)} fusion(f32[64,2048]{1,0:T(8,128)} %copy.56, f32[64,2048]{1,0:T(8,128)} %copy.55, bf16[1,128,2048]{2,1,0:T(8,128)(2,1)} %param.6), kind=kLoop, calls=%fused_computation.9 | loop fusion | flops 1048576 | bytes 2097152 | tf_op jit(solution)/shard_map/convert_element_type | solution.py:85
  124.7 1.5 collective-permute-start.2
  126.2 1.1 copy.53
  127.3 2.3 %copy.54 = f32[1,64,2048]{2,1,0:T(8,128)} copy(f32[1,64,2048]{1,2,0:T(8,128)} %bitcast.67) | data formatting | bytes 1048576 | tf_op jit(solution)/shard_map/concatenate | solution.py:50
  129.6 3.5 %fusion.6 = f32[128,16,64]{2,1,0:T(8,128)S(1)} fusion(bf16[191,128,16]{0,2,1:T(8,128)(2,1)S(1)} %bitcast.61, bf16[128,64,191]{2,1,0:T(8,128)(2,1)} %copy.43), kind=kOutput, calls=%fused_computation.20 | convolution fusion | flops 50069504 | bytes 4435968 | tf_op jit(solution)/shard_map/gts,sgc->tgc/dot_general | solution.py:35
  133.2 0.0 copy-done.7
  133.2 0.0 copy-done.8
  133.2 0.9 fusion.1
  134.1 1.2 fusion.7
  135.3 0.3 copy.46
  135.6 0.3 copy.47
  135.9 3.8 %all-reduce.6.cloned.1.call-done = f32[128,128]{0,1:T(8,128)} async-done(((f32[128,128]{0,1:T(8,128)}), f32[128,128]{0,1:T(8,128)}) %all-reduce.6.cloned.1.call-update) | async-done | bytes 65552 | tf_op jit(solution)/shard_map/psum | solution.py:103
  139.7 1.5 multiply_reduce_fusion
  141.2 1.9 %fusion = bf16[1,128,2048]{2,1,0:T(8,128)(2,1)} fusion(f32[1,64,2048]{2,1,0:T(8,128)S(1)} %copy.47, f32[1,64,2048]{2,1,0:T(8,128)S(1)} %copy.46, bf16[1,128,2048]{2,1,0:T(8,128)(2,1)} %param.8), kind=kLoop, calls=%fused_computation.3 | loop fusion | flops 1048576 | bytes 2097152 | tf_op jit(solution)/shard_map/convert_element_type | solution.py:75
  143.1 22.0 %psum.15 = f32[]{:T(128)} all-reduce(f32[]{:T(128)} %multiply_reduce_fusion), channel_id=1, replica_groups=mesh['ctx'=4,'tp'=4,'pp'=2] {'tp','pp'}, use_global_device_ids=true, to_apply=%region_4.0 | all-reduce | flops 1 | bytes 8 | tf_op jit(solution)/shard_map/psum | solution.py:104
  165.9 0.8 multiply_bitcast_fusion
  166.7 0.7 copy.61
  167.4 1.9 %copy.68 = bf16[1,128,2048]{2,1,0:T(8,128)(2,1)} copy(bf16[1,128,2048]{2,1,0:T(8,128)(2,1)} %bitcast.22) | data formatting | bytes 1048576
  (25 shorter events, 0.1 us)
Async XLA Ops:
  7.2 9.1 %copy-start.9 = (f32[1,128,128]{2,1,0:T(8,128)S(1)}, f32[1,128,128]{2,1,0:T(8,128)}, u32[]{:S(2)}) copy-start(f32[1,128,128]{2,1,0:T(8,128)} %param.9) | copy-start | bytes 196612
  7.2 132.6 %all-reduce.6.cloned.1.call-start = ((), (), s32[]{:S(2)}) async-start(), calls=%async_computation | async-start | bytes 131072 | tf_op jit(solution)/shard_map/psum | solution.py:103
  8.6 1.0 copy-start.3
  9.5 35.6 %collective-permute-start = (bf16[127,2048]{1,0:T(8,128)(2,1)}, bf16[127,2048]{1,0:T(8,128)(2,1)}, u32[]{:S(2)}, u32[]{:S(2)}) collective-permute-start(bf16[127,2048]{1,0:T(8,128)(2,1)} %slice_bitcast_fusion.1), channel_id=1, source_target_pairs={{0,8},{8,16},{16,24},{1,9},{9,17},{17,25},{2,10},{10,18},{18,26},{... | collective-permute-start | bytes 1560584 | tf_op jit(solution)/shard_map/ppermute | solution.py:19
  14.0 5.3 %copy-start.1 = (bf16[1,128,2048]{2,1,0:T(8,128)(2,1)}, bf16[1,128,2048]{2,1,0:T(8,128)(2,1)S(1)}, u32[]{:S(2)}) copy-start(bf16[1,128,2048]{2,1,0:T(8,128)(2,1)S(1)} %mul.35) | copy-start | bytes 1572868
  14.9 89.8 %collective-permute-start.1 = (bf16[127,2048]{1,0:T(8,128)(2,1)}, bf16[127,2048]{1,0:T(8,128)(2,1)}, u32[]{:S(2)}, u32[]{:S(2)}) collective-permute-start(bf16[127,2048]{1,0:T(8,128)(2,1)} %slice_bitcast_fusion), channel_id=1, source_target_pairs={{8,0},{16,8},{24,16},{9,1},{17,9},{25,17},{10,2},{18,10},{26,18},{... | collective-permute-start | bytes 1560584 | tf_op jit(solution)/shard_map/ppermute | solution.py:19
  45.1 2.2 %copy-start.5 = (bf16[1,64,2048]{1,2,0:T(8,128)(2,1)S(1)}, bf16[1,64,2048]{1,2,0:T(8,128)(2,1)}, u32[]{:S(2)}) copy-start(bf16[1,64,2048]{1,2,0:T(8,128)(2,1)} %copy.57) | copy-start | bytes 786436
  72.2 3.7 %copy-start.4 = (bf16[1,64,2048]{1,2,0:T(8,128)(2,1)S(1)}, bf16[1,64,2048]{1,2,0:T(8,128)(2,1)}, u32[]{:S(2)}) copy-start(bf16[1,64,2048]{1,2,0:T(8,128)(2,1)} %copy.59) | copy-start | bytes 786436
  100.9 3.9 %copy-start.2 = (bf16[1,128,2048]{2,1,0:T(8,128)(2,1)S(1)}, bf16[1,128,2048]{2,1,0:T(8,128)(2,1)}, u32[]{:S(2)}) copy-start(bf16[1,128,2048]{2,1,0:T(8,128)(2,1)} %copy-done.1) | copy-start | bytes 1572868
  124.7 42.7 %collective-permute-start.2 = (bf16[128,2048]{1,0:T(8,128)(2,1)}, bf16[128,2048]{1,0:T(8,128)(2,1)}, u32[]{:S(2)}, u32[]{:S(2)}) collective-permute-start(bf16[128,2048]{1,0:T(8,128)(2,1)} %fusion.2), channel_id=1, source_target_pairs={{1,0},{3,2},{5,4},{7,6},{9,8},{11,10},{13,12},{15,14},{17,16},{19,... | collective-permute-start | bytes 1572872 | tf_op jit(solution)/shard_map/ppermute | solution.py:19
  129.6 3.6 %copy-start.6 = (bf16[1,128,2048]{2,1,0:T(8,128)(2,1)S(1)}, bf16[1,128,2048]{2,1,0:T(8,128)(2,1)}, u32[]{:S(2)}) copy-start(bf16[1,128,2048]{2,1,0:T(8,128)(2,1)} %param.7) | copy-start | bytes 1572868
  129.6 3.6 %copy-start.7 = (f32[1,64,2048]{2,1,0:T(8,128)S(1)}, f32[1,64,2048]{2,1,0:T(8,128)}, u32[]{:S(2)}) copy-start(f32[1,64,2048]{2,1,0:T(8,128)} %copy.53) | copy-start | bytes 1572868
  129.6 3.6 %copy-start.8 = (f32[1,64,2048]{2,1,0:T(8,128)S(1)}, f32[1,64,2048]{2,1,0:T(8,128)}, u32[]{:S(2)}) copy-start(f32[1,64,2048]{2,1,0:T(8,128)} %copy.54) | copy-start | bytes 1572868
  129.6 4.5 %copy-start = (bf16[128,64,191]{2,1,0:T(8,128)(2,1)S(1)}, bf16[128,64,191]{2,1,0:T(8,128)(2,1)}, u32[]{:S(2)}) copy-start(bf16[128,64,191]{2,1,0:T(8,128)(2,1)} %copy.43) | copy-start | bytes 9388036
Sparse Core Ops, SparseCore 0:
  104.8 34.8 all-reduce.5
where the time goes:
time: 177 us; the launch traced here: 176 us
  local copies, waits for them, and re-layouts  86.3 us (49%)
  matrix products  22.2 us (13%)
  blocking collectives  22 us (12%)
  other arithmetic  20.9 us (12%)
  between operations  15 us (8%)
  starting transfers between devices  5.91 us (3%)
  waiting for transfers between devices  3.82 us (2%)
    reshape x4, local copies, waits for them, and re-layouts, per_device(): flat = pairs.reshape(groups_here, block_rows * span)  31.3 us
    psum x1, blocking collectives, per_device(): norm_sq = lax.psum(jnp.sum(summed * summed), ('tp', 'pp'))  22 us
    reshape x4, local copies, waits for them, and re-layouts, build_kernel(): return tiled[:, :row_count * span].reshape(groups_here, row_count, span)  21.4 us
    dot_general x4, matrix products, apply_kernel(): jnp.einsum('gts,sgc->tgc', kernel, pieces, preferred_element_type=jnp.flo...  13.2 us
    concatenate x2, local copies, waits for them, and re-layouts, per_device(): jnp.concatenate([flat, jnp.zeros((groups_here, block_rows), jnp.float32)]...  9.51 us
    dot_general x2, matrix products, per_device(): jnp.einsum('tgc,sgc->gts', grad_block, window, preferred_element_type=jnp...  9.08 us
    reduce_sum x2, other arithmetic, per_device(): skewed = flat.reshape(groups_here, block_rows, span + 1).sum(axis=1)  6.3 us
    ppermute x3, starting transfers between devices, from_behind(): return lax.ppermute(block, axis, route)  5.87 us
  transfers between devices with their start and end apart: 4, of which 1 were waited for; matrix products, arithmetic and copies ran while one was open for 71% of the time, Pallas kernels for 0%

commit v1 on v0

v1 whole, which is shorter than its diff:
```python
import functools
import math

import jax
import jax.numpy as jnp
from jax import lax
from jax.experimental import pallas as pl
from jax.experimental.pallas import tpu as pltpu
from jax.sharding import PartitionSpec as P

TAPS = 128
GROUP = 16
LANES = 128
PER = LANES // GROUP
BLK = 32
WIDTH = 256
MESH = pl.DeviceIdType.MESH
F32 = jnp.float32
BF16 = jnp.bfloat16


def dot(lhs, rhs, contract):
    return lax.dot_general(lhs, rhs, (contract, ((), ())), preferred_element_type=F32)


def kernel(
    sizes, chunk, clip_level,
    q_hbm, k_hbm, v_hbm, c_hbm, f_ref,
    gq_hbm, gk_hbm, ho_hbm, gf_ref,
    qv, kv, vv, cv, wext, pext, gq, gk, dv, toep_b, toep_f, taps, raws, norms,
    in_sem, out_sem, w_send, w_recv, p_send, p_recv, d_send, d_recv,
    r_send, r_recv, n_send, n_recv,
):
    n_ctx, n_tp, n_pp = sizes
    ctx, tp, pp = (lax.axis_index(a) for a in ("ctx", "tp", "pp"))
    n_chunks, rows, _ = qv.shape
    groups = f_ref.shape[1]
    n_quad = n_tp * n_pp
    me = pp * n_tp + tp
    has_next, has_prev = ctx < n_ctx - 1, ctx > 0
    span = BLK + TAPS
    blocks = rows // BLK
    subs = chunk // LANES

    def each(count, body):
        def step(i, _):
            body(i)
            return 0
        lax.fori_loop(0, count, step, 0)

    def ctx_peer(d):
        return {"ctx": lax.rem(ctx + d, n_ctx)}

    def quad(d):
        other = lax.rem(me + d, n_quad)
        return {"tp": lax.rem(other, n_tp), "pp": other // n_tp}

    barrier = pltpu.get_barrier_semaphore()
    each(n_ctx - 1, lambda d: pl.semaphore_signal(
        barrier, inc=1, device_id=ctx_peer(d + 1), device_id_type=MESH))
    each(n_quad - 1, lambda d: pl.semaphore_signal(
        barrier, inc=1, device_id=quad(d + 1), device_id_type=MESH))

    def load(which, hbm, vmem, i):
        cols = pl.ds(pl.multiple_of(i * chunk, chunk), chunk)
        return pltpu.make_async_copy(hbm.at[0, :, cols], vmem.at[i], in_sem.at[which, i])

    def store(which, vmem, hbm, i):
        cols = pl.ds(pl.multiple_of(i * chunk, chunk), chunk)
        return pltpu.make_async_copy(vmem.at[i], hbm.at[0, :, cols], out_sem.at[which, i])

    loads = ((c_hbm, cv), (q_hbm, qv), (k_hbm, kv), (v_hbm, vv))

    def start_loads(i):
        for which, (hbm, vmem) in enumerate(loads):
            load(which, hbm, vmem, i).start()
    each(n_chunks, start_loads)

    rounded = f_ref[0].astype(BF16)
    flip = (
        lax.broadcasted_iota(jnp.int32, (TAPS, TAPS), 0)
        + lax.broadcasted_iota(jnp.int32, (TAPS, TAPS), 1)
        == TAPS - 1
    )
    taps[0] = rounded.astype(F32)
    taps[1] = dot(rounded, flip.astype(F32).astype(BF16), ((1,), (0,)))

    def toeplitz(which, first, out, i):
        eight = taps[which, pl.ds(pl.multiple_of(i * PER, PER), PER), :]
        pieces = []
        for g in range(PER):
            row = jnp.concatenate([eight[g : g + 1], jnp.zeros((1, WIDTH - TAPS), F32)], axis=1)
            wide = jnp.broadcast_to(row, (BLK, WIDTH))
            pieces.append(pltpu.roll(wide, first, 1, stride=1, stride_axis=0).astype(BF16))
        out[i] = jnp.concatenate(pieces, axis=0)

    each(groups // PER, lambda i: toeplitz(0, 0, toep_b, i))

    @pl.when(jnp.logical_not(has_next))
    def _():
        wext[:, rows:, :] = jnp.zeros((n_chunks, rows, chunk), BF16)

    @pl.when(jnp.logical_not(has_prev))
    def _():
        pext[:, :rows, :] = jnp.zeros((n_chunks, rows, chunk), BF16)

    @pl.when(pp == n_pp - 1)
    def _():
        dv[n_chunks] = jnp.zeros((rows, chunk), BF16)

        def clear(i):
            cols = pl.ds(pl.multiple_of(i * chunk, chunk), chunk)
            pltpu.make_async_copy(
                dv.at[n_chunks], ho_hbm.at[0, :, cols], out_sem.at[2, i]).start()
        each(n_chunks, clear)

    pl.semaphore_wait(barrier, n_ctx - 1 + n_quad - 1)

    def send_w(i):
        return pltpu.make_async_remote_copy(
            src_ref=wext.at[i, pl.ds(0, rows)], dst_ref=wext.at[i, pl.ds(rows, rows)],
            send_sem=w_send.at[i], recv_sem=w_recv.at[i],
            device_id={"ctx": ctx - 1}, device_id_type=MESH)

    def send_p(i):
        return pltpu.make_async_remote_copy(
            src_ref=pext.at[i, pl.ds(rows, rows)], dst_ref=pext.at[i, pl.ds(0, rows)],
            send_sem=p_send.at[i], recv_sem=p_recv.at[i],
            device_id={"ctx": ctx + 1}, device_id_type=MESH)

    def send_d(i):
        cols = pl.ds(pl.multiple_of(i * chunk, chunk), chunk)
        return pltpu.make_async_remote_copy(
            src_ref=dv.at[i], dst_ref=ho_hbm.at[0, :, cols],
            send_sem=d_send.at[i], recv_sem=d_recv.at[i],
            device_id={"pp": pp - 1}, device_id_type=MESH)

    def elementwise(i):
        load(0, c_hbm, cv, i).wait()
        load(1, q_hbm, qv, i).wait()
        wext[i, :rows, :] = (cv[i].astype(F32) * qv[i].astype(F32)).astype(BF16)

        @pl.when(has_prev)
        def _():
            send_w(i).start()
        load(2, k_hbm, kv, i).wait()
        load(3, v_hbm, vv, i).wait()
        pext[i, rows:, :] = (kv[i].astype(F32) * vv[i].astype(F32)).astype(BF16)

        @pl.when(has_next)
        def _():
            send_p(i).start()
    each(n_chunks, elementwise)

    owner = lax.broadcasted_iota(jnp.int32, (BLK, LANES), 1) // GROUP

    def filtered(toep, ext, i, s, a):
        mat = toep[i * subs + s, :, :span]
        window = ext[i, a * BLK : a * BLK + span, s * LANES : (s + 1) * LANES]
        full = dot(mat, window, ((1,), (0,)))
        result = full[:BLK]
        for g in range(1, PER):
            result = jnp.where(owner == g, full[g * BLK : (g + 1) * BLK], result)
        return result

    def backward(i):
        @pl.when(has_next)
        def _():
            send_w(i).wait_recv()
        for s in range(subs):
            cols = slice(s * LANES, (s + 1) * LANES)
            for a in range(blocks):
                here = slice(a * BLK, (a + 1) * BLK)
                dprod = filtered(toep_b, wext, i, s, a)
                dv[i, here, cols] = (dprod * kv[i, here, cols].astype(F32)).astype(BF16)
                gk[i, here, cols] = (dprod * vv[i, here, cols].astype(F32)).astype(BF16)

        @pl.when(pp > 0)
        def _():
            send_d(i).start()
        store(0, gk, gk_hbm, i).start()
    each(n_chunks, backward)

    place = lax.broadcasted_iota(jnp.int32, (8, WIDTH), 0)

    def tap_grad(i):
        for s in range(subs):
            cols = slice(s * LANES, (s + 1) * LANES)
            left, right = [], []
            for a in range(blocks):
                own = pext[i, rows + a * BLK : rows + (a + 1) * BLK, cols]
                left.append(jnp.concatenate(
                    [jnp.where(owner == g, own, jnp.zeros_like(own)) for g in range(PER)], axis=0))
                right.append(wext[i, a * BLK : a * BLK + span, cols])
            pairs = dot(
                jnp.concatenate(left, axis=1), jnp.concatenate(right, axis=1), ((1,), (1,)))
            pairs = jnp.concatenate(
                [pairs, jnp.zeros((PER * BLK, WIDTH - span), F32)], axis=1)
            sums = []
            for g in range(PER):
                total = pairs[g * BLK : g * BLK + 8]
                for b in range(8, BLK, 8):
                    total = total + pltpu.roll(
                        pairs[g * BLK + b : g * BLK + b + 8], WIDTH - b, 1)
                for bit in (1, 2, 4):
                    moved = pltpu.roll(total, WIDTH - bit, 1)
                    total = jnp.where((place & bit) != 0, moved, total)
                sums.append(jnp.sum(total[:, :TAPS], axis=0, keepdims=True))
            at = pl.ds(pl.multiple_of((i * subs + s) * PER, PER), PER)
            raws[ctx, at, :] = jnp.concatenate(sums, axis=0)
    each(n_chunks, tap_grad)

    def send_r(d):
        return pltpu.make_async_remote_copy(
            src_ref=raws.at[ctx], dst_ref=raws.at[ctx],
            send_sem=r_send.at[d], recv_sem=r_recv.at[d],
            device_id=ctx_peer(d + 1), device_id_type=MESH)

    def recv_r(d):
        slot = lax.rem(ctx + n_ctx - 1 - d, n_ctx)
        return pltpu.make_async_remote_copy(
            src_ref=raws.at[slot], dst_ref=raws.at[slot],
            send_sem=r_send.at[d], recv_sem=r_recv.at[d],
            device_id=ctx_peer(d + 1), device_id_type=MESH)
    each(n_ctx - 1, lambda d: send_r(d).start())

    each(groups // PER, lambda i: toeplitz(1, 1, toep_f, i))

    def forward(i):
        @pl.when(has_prev)
        def _():
            send_p(i).wait_recv()
        for s in range(subs):
            cols = slice(s * LANES, (s + 1) * LANES)
            for a in range(blocks):
                here = slice(a * BLK, (a + 1) * BLK)
                mixed = filtered(toep_f, pext, i, s, a)
                gq[i, here, cols] = (mixed * cv[i, here, cols].astype(F32)).astype(BF16)
        store(1, gq, gq_hbm, i).start()

    each(n_chunks, forward)

    each(n_ctx - 1, lambda d: recv_r(d).wait_recv())
    summed = raws[0]
    for d in range(1, n_ctx):
        summed = summed + raws[d]
    squares = jnp.sum(summed * summed, axis=0, keepdims=True)
    norms[me] = jnp.broadcast_to(squares, (8, TAPS))

    def send_n(d):
        return pltpu.make_async_remote_copy(
            src_ref=norms.at[me], dst_ref=norms.at[me],
            send_sem=n_send.at[d], recv_sem=n_recv.at[d],
            device_id=quad(d + 1), device_id_type=MESH)

    def recv_n(d):
        slot = lax.rem(me + n_quad - 1 - d, n_quad)
        return pltpu.make_async_remote_copy(
            src_ref=norms.at[slot], dst_ref=norms.at[slot],
            send_sem=n_send.at[d], recv_sem=n_recv.at[d],
            device_id=quad(d + 1), device_id_type=MESH)
    each(n_quad - 1, lambda d: send_n(d).start())
    each(n_quad - 1, lambda d: recv_n(d).wait_recv())
    squares = norms[0]
    for d in range(1, n_quad):
        squares = squares + norms[d]
    norm_sq = jnp.sum(squares[:1], axis=1, keepdims=True)
    factor = jnp.minimum(1.0, clip_level / (jnp.sqrt(norm_sq) + 1e-6))
    gf_ref[0] = summed * factor

    each(n_ctx - 1, lambda d: send_r(d).wait_send())
    each(n_quad - 1, lambda d: send_n(d).wait_send())

    def drain(i):
        store(0, gk, gk_hbm, i).wait()
        store(1, gq, gq_hbm, i).wait()

        @pl.when(has_prev)
        def _():
            send_w(i).wait_send()

        @pl.when(has_next)
        def _():
            send_p(i).wait_send()

        @pl.when(pp > 0)
        def _():
            send_d(i).wait_send()

        @pl.when(pp < n_pp - 1)
        def _():
            send_d(i).wait_recv()

        @pl.when(pp == n_pp - 1)
        def _():
            cols = pl.ds(pl.multiple_of(i * chunk, chunk), chunk)
            pltpu.make_async_copy(
                dv.at[n_chunks], ho_hbm.at[0, :, cols], out_sem.at[2, i]).wait()
    each(n_chunks, drain)


def per_device(sizes, queries, key_feats, value_feats, cotangent, filters):
    n_ctx, n_tp, n_pp = sizes
    _, rows, channels = queries.shape
    groups = filters.shape[1]
    chunk = math.gcd(channels, 256)
    n_chunks = channels // chunk
    n_quad = n_tp * n_pp
    clip_level = 0.25 * math.sqrt(n_pp * n_tp * groups * TAPS)
    block = jax.ShapeDtypeStruct(queries.shape, BF16)
    own = pltpu.VMEM((n_chunks, rows, chunk), BF16)
    double = pltpu.VMEM((n_chunks, 2 * rows, chunk), BF16)
    toep = pltpu.VMEM((groups // PER, PER * BLK, WIDTH), BF16)
    dma = pltpu.SemaphoreType.DMA
    per_chunk = dma((n_chunks,))
    hbm = pl.BlockSpec(memory_space=pl.ANY)
    vmem = pl.BlockSpec(memory_space=pltpu.VMEM)
    return pl.pallas_call(
        functools.partial(kernel, sizes, chunk, clip_level),
        out_shape=(block, block, block, jax.ShapeDtypeStruct(filters.shape, F32)),
        in_specs=[hbm] * 4 + [vmem],
        out_specs=(hbm, hbm, hbm, vmem),
        scratch_shapes=[
            own, own, own, own, double, double, own, own,
            pltpu.VMEM((n_chunks + 1, rows, chunk), BF16),
            toep, toep,
            pltpu.VMEM((2, groups, TAPS), F32),
            pltpu.VMEM((n_ctx, groups, TAPS), F32),
            pltpu.VMEM((n_quad, 8, TAPS), F32),
            dma((4, n_chunks)), dma((3, n_chunks)),
            per_chunk, per_chunk, per_chunk, per_chunk, per_chunk, per_chunk,
            dma((n_ctx,)), dma((n_ctx,)), dma((n_quad,)), dma((n_quad,)),
        ],
        compiler_params=pltpu.CompilerParams(
            collective_id=0, has_side_effects=True, vmem_limit_bytes=48 << 20),
    )(queries, key_feats, value_feats, cotangent, filters)


def solution(mesh):
    sizes = tuple(mesh.shape[a] for a in ("ctx", "tp", "pp"))
    tokens = P("pp", "ctx", "tp")
    taps = P("pp", "tp", None)
    return jax.shard_map(
        functools.partial(per_device, sizes),
        mesh=mesh,
        in_specs=(tokens, tokens, tokens, tokens, taps),
        out_specs=(tokens, tokens, tokens, taps),
        check_vma=False,
    )
```

time: 177 us -> 38.2 us (0.22)
  the two profiles are of different devices: /device:TPU:0 before, /device:TPU:1 now
where the time goes in v1:
time: 38.2 us; the launch traced here: 37.9 us
  Pallas kernels  29.2 us (76%)
  local copies, waits for them, and re-layouts  8.01 us (21%)
  between operations  0.65 us (2%)
    pallas_call x1, Pallas kernels, per_device(): pl.pallas_call(functools.partial(kernel, sizes, chunk, clip_level), out_s...  29.2 us
    unnamed x14, local copies, waits for them, and re-layouts  8.01 us

profile of v1, /device:TPU:1, one launch (start us, length us, event | category | flops | bytes accessed | tf_op | source)
XLA Modules:
  0.0 37.9 jit_solution(13538699423798937085)
XLA Ops:
  0.6 0.0 copy-start
  0.6 1.0 %copy-done = bf16[1,128,2048]{2,1,0:T(8,128)(2,1)S(1)} copy-done((bf16[1,128,2048]{2,1,0:T(8,128)(2,1)S(1)}, bf16[1,128,2048]{2,1,0:T(8,128)(2,1)}, u32[]{:S(2)}) %copy-start) | copy-done | bytes 524312
  1.7 0.0 copy-start.1
  1.7 1.0 %copy-done.1 = bf16[1,128,2048]{2,1,0:T(8,128)(2,1)S(1)} copy-done((bf16[1,128,2048]{2,1,0:T(8,128)(2,1)S(1)}, bf16[1,128,2048]{2,1,0:T(8,128)(2,1)}, u32[]{:S(2)}) %copy-start.1) | copy-done | bytes 524312
  2.7 0.0 copy-start.2
  2.7 1.0 %copy-done.2 = bf16[1,128,2048]{2,1,0:T(8,128)(2,1)S(1)} copy-done((bf16[1,128,2048]{2,1,0:T(8,128)(2,1)S(1)}, bf16[1,128,2048]{2,1,0:T(8,128)(2,1)}, u32[]{:S(2)}) %copy-start.2) | copy-done | bytes 524312
  3.8 0.0 copy-start.3
  3.8 1.0 %copy-done.3 = bf16[1,128,2048]{2,1,0:T(8,128)(2,1)S(1)} copy-done((bf16[1,128,2048]{2,1,0:T(8,128)(2,1)S(1)}, bf16[1,128,2048]{2,1,0:T(8,128)(2,1)}, u32[]{:S(2)}) %copy-start.3) | copy-done | bytes 524312
  4.8 0.0 copy-start.4
  4.8 0.8 %copy-done.4 = f32[1,128,128]{2,1,0:T(8,128)S(1)} copy-done((f32[1,128,128]{2,1,0:T(8,128)S(1)}, f32[1,128,128]{2,1,0:T(8,128)}, u32[]{:S(2)}) %copy-start.4) | copy-done | bytes 65560
  5.6 29.2 %shard_map.84 = (bf16[1,128,2048]{2,1,0:T(8,128)(2,1)S(1)}, bf16[1,128,2048]{2,1,0:T(8,128)(2,1)S(1)}, bf16[1,128,2048]{2,1,0:T(8,128)(2,1)S(1)}, f32[1,128,128]{2,1,0:T(8,128)S(1)}) custom-call(bf16[1,128,2048]{2,1,0:T(8,128)(2,1)S(1)} %copy-done, bf16[1,128,2048]{2,1,0:T(8,128)(2,1)S(1)} %copy-done.1, bf16[1,128,2048]{2,1,0:T(8,128)(2,1)S(1)} %copy-done.2, ...), custom_call_target="tpu_custom_call" | custom-call | tf_op jit(solution)/shard_map/pallas_call | solution.py:318
  34.9 0.8 %copy.13 = bf16[1,128,2048]{2,1,0:T(8,128)(2,1)} copy(bf16[1,128,2048]{2,1,0:T(8,128)(2,1)S(1)} %get-tuple-element.8) | data formatting | bytes 1048576
  35.7 0.8 %copy.14 = bf16[1,128,2048]{2,1,0:T(8,128)(2,1)} copy(bf16[1,128,2048]{2,1,0:T(8,128)(2,1)S(1)} %get-tuple-element.9) | data formatting | bytes 1048576
  36.5 0.8 %copy.15 = bf16[1,128,2048]{2,1,0:T(8,128)(2,1)} copy(bf16[1,128,2048]{2,1,0:T(8,128)(2,1)S(1)} %get-tuple-element.10) | data formatting | bytes 1048576
  37.3 0.6 %copy.16 = f32[1,128,128]{2,1,0:T(8,128)} copy(f32[1,128,128]{2,1,0:T(8,128)S(1)} %get-tuple-element.11) | data formatting | bytes 131072
Async XLA Ops:
  0.6 1.0 %copy-start = (bf16[1,128,2048]{2,1,0:T(8,128)(2,1)S(1)}, bf16[1,128,2048]{2,1,0:T(8,128)(2,1)}, u32[]{:S(2)}) copy-start(bf16[1,128,2048]{2,1,0:T(8,128)(2,1)} %q_hbm.1) | copy-start | bytes 1572868
  1.7 1.0 %copy-start.1 = (bf16[1,128,2048]{2,1,0:T(8,128)(2,1)S(1)}, bf16[1,128,2048]{2,1,0:T(8,128)(2,1)}, u32[]{:S(2)}) copy-start(bf16[1,128,2048]{2,1,0:T(8,128)(2,1)} %k_hbm.1) | copy-start | bytes 1572868
  2.7 1.0 %copy-start.2 = (bf16[1,128,2048]{2,1,0:T(8,128)(2,1)S(1)}, bf16[1,128,2048]{2,1,0:T(8,128)(2,1)}, u32[]{:S(2)}) copy-start(bf16[1,128,2048]{2,1,0:T(8,128)(2,1)} %v_hbm.1) | copy-start | bytes 1572868
  3.8 1.0 %copy-start.3 = (bf16[1,128,2048]{2,1,0:T(8,128)(2,1)S(1)}, bf16[1,128,2048]{2,1,0:T(8,128)(2,1)}, u32[]{:S(2)}) copy-start(bf16[1,128,2048]{2,1,0:T(8,128)(2,1)} %c_hbm.1) | copy-start | bytes 1572868
  4.8 0.8 %copy-start.4 = (f32[1,128,128]{2,1,0:T(8,128)S(1)}, f32[1,128,128]{2,1,0:T(8,128)}, u32[]{:S(2)}) copy-start(f32[1,128,128]{2,1,0:T(8,128)} %f_ref.1) | copy-start | bytes 196612

commit v2 on v1

--- a/solution.py
+++ b/solution.py
@@ -25,16 +25,16 @@
 
 def kernel(
     sizes, chunk, clip_level,
-    q_hbm, k_hbm, v_hbm, c_hbm, f_ref,
-    gq_hbm, gk_hbm, ho_hbm, gf_ref,
-    qv, kv, vv, cv, wext, pext, gq, gk, dv, toep_b, toep_f, taps, raws, norms,
-    in_sem, out_sem, w_send, w_recv, p_send, p_recv, d_send, d_recv,
+    q_hbm, k_hbm, v_hbm, c_hbm, f_hbm,
+    gq, gk, ho, gf_ref,
+    qv, kv, vv, cv, fv, wext, pext, dv, toep_b, toep_f, taps, raws, norms,
+    in_sem, f_sem, w_send, w_recv, p_send, p_recv, d_send, d_recv,
     r_send, r_recv, n_send, n_recv,
 ):
     n_ctx, n_tp, n_pp = sizes
     ctx, tp, pp = (lax.axis_index(a) for a in ("ctx", "tp", "pp"))
     n_chunks, rows, _ = qv.shape
-    groups = f_ref.shape[1]
+    groups = fv.shape[0]
     n_quad = n_tp * n_pp
     me = pp * n_tp + tp
     has_next, has_prev = ctx < n_ctx - 1, ctx > 0
@@ -65,18 +65,17 @@
         cols = pl.ds(pl.multiple_of(i * chunk, chunk), chunk)
         return pltpu.make_async_copy(hbm.at[0, :, cols], vmem.at[i], in_sem.at[which, i])
 
-    def store(which, vmem, hbm, i):
-        cols = pl.ds(pl.multiple_of(i * chunk, chunk), chunk)
-        return pltpu.make_async_copy(vmem.at[i], hbm.at[0, :, cols], out_sem.at[which, i])
-
     loads = ((c_hbm, cv), (q_hbm, qv), (k_hbm, kv), (v_hbm, vv))
 
     def start_loads(i):
         for which, (hbm, vmem) in enumerate(loads):
             load(which, hbm, vmem, i).start()
+    load_taps = pltpu.make_async_copy(f_hbm.at[0], fv, f_sem)
+    load_taps.start()
     each(n_chunks, start_loads)
-
-    rounded = f_ref[0].astype(BF16)
+    load_taps.wait()
+
+    rounded = fv[...].astype(BF16)
     flip = (
         lax.broadcasted_iota(jnp.int32, (TAPS, TAPS), 0)
         + lax.broadcasted_iota(jnp.int32, (TAPS, TAPS), 1)
@@ -106,13 +105,7 @@
 
     @pl.when(pp == n_pp - 1)
     def _():
-        dv[n_chunks] = jnp.zeros((rows, chunk), BF16)
-
-        def clear(i):
-            cols = pl.ds(pl.multiple_of(i * chunk, chunk), chunk)
-            pltpu.make_async_copy(
-                dv.at[n_chunks], ho_hbm.at[0, :, cols], out_sem.at[2, i]).start()
-        each(n_chunks, clear)
+        ho[...] = jnp.zeros_like(ho)
 
     pl.semaphore_wait(barrier, n_ctx - 1 + n_quad - 1)
 
@@ -131,7 +124,7 @@
     def send_d(i):
         cols = pl.ds(pl.multiple_of(i * chunk, chunk), chunk)
         return pltpu.make_async_remote_copy(
-            src_ref=dv.at[i], dst_ref=ho_hbm.at[0, :, cols],
+            src_ref=dv.at[i], dst_ref=ho.at[0, :, cols],
             send_sem=d_send.at[i], recv_sem=d_recv.at[i],
             device_id={"pp": pp - 1}, device_id_type=MESH)
 
@@ -151,6 +144,9 @@
         def _():
             send_p(i).start()
     each(n_chunks, elementwise)
+
+    def lanes_of(i, s):
+        return pl.ds(pl.multiple_of(i * chunk + s * LANES, LANES), LANES)
 
     owner = lax.broadcasted_iota(jnp.int32, (BLK, LANES), 1) // GROUP
 
@@ -173,12 +169,11 @@
                 here = slice(a * BLK, (a + 1) * BLK)
                 dprod = filtered(toep_b, wext, i, s, a)
                 dv[i, here, cols] = (dprod * kv[i, here, cols].astype(F32)).astype(BF16)
-                gk[i, here, cols] = (dprod * vv[i, here, cols].astype(F32)).astype(BF16)
+                gk[0, here, lanes_of(i, s)] = (dprod * vv[i, here, cols].astype(F32)).astype(BF16)
 
         @pl.when(pp > 0)
         def _():
             send_d(i).start()
-        store(0, gk, gk_hbm, i).start()
     each(n_chunks, backward)
 
     place = lax.broadcasted_iota(jnp.int32, (8, WIDTH), 0)
@@ -235,8 +230,7 @@
             for a in range(blocks):
                 here = slice(a * BLK, (a + 1) * BLK)
                 mixed = filtered(toep_f, pext, i, s, a)
-                gq[i, here, cols] = (mixed * cv[i, here, cols].astype(F32)).astype(BF16)
-        store(1, gq, gq_hbm, i).start()
+                gq[0, here, lanes_of(i, s)] = (mixed * cv[i, here, cols].astype(F32)).astype(BF16)
 
     each(n_chunks, forward)
 
@@ -272,9 +266,6 @@
     each(n_quad - 1, lambda d: send_n(d).wait_send())
 
     def drain(i):
-        store(0, gk, gk_hbm, i).wait()
-        store(1, gq, gq_hbm, i).wait()
-
         @pl.when(has_prev)
         def _():
             send_w(i).wait_send()
@@ -290,13 +281,18 @@
         @pl.when(pp < n_pp - 1)
         def _():
             send_d(i).wait_recv()
-
-        @pl.when(pp == n_pp - 1)
-        def _():
-            cols = pl.ds(pl.multiple_of(i * chunk, chunk), chunk)
-            pltpu.make_async_copy(
-                dv.at[n_chunks], ho_hbm.at[0, :, cols], out_sem.at[2, i]).wait()
     each(n_chunks, drain)
+
+
+def write_back(*refs):
+    n = (len(refs) - 1) // 2
+    copies = [
+        pltpu.make_async_copy(refs[i], refs[n + i], refs[2 * n].at[i]) for i in range(n)
+    ]
+    for copy in copies:
+        copy.start()
+    for copy in copies:
+        copy.wait()
 
 
 def per_device(sizes, queries, key_feats, value_feats, cotangent, filters):
@@ -313,27 +309,35 @@
     toep = pltpu.VMEM((groups // PER, PER * BLK, WIDTH), BF16)
     dma = pltpu.SemaphoreType.DMA
     per_chunk = dma((n_chunks,))
-    hbm = pl.BlockSpec(memory_space=pl.ANY)
+    hbm = pl.BlockSpec(memory_space=pltpu.HBM)
     vmem = pl.BlockSpec(memory_space=pltpu.VMEM)
-    return pl.pallas_call(
+    out_shape = (block, block, block, jax.ShapeDtypeStruct(filters.shape, F32))
+    results = pl.pallas_call(
         functools.partial(kernel, sizes, chunk, clip_level),
-        out_shape=(block, block, block, jax.ShapeDtypeStruct(filters.shape, F32)),
-        in_specs=[hbm] * 4 + [vmem],
-        out_specs=(hbm, hbm, hbm, vmem),
+        out_shape=out_shape,
+        in_specs=[hbm] * 5,
+        out_specs=(vmem,) * 4,
         scratch_shapes=[
-            own, own, own, own, double, double, own, own,
-            pltpu.VMEM((n_chunks + 1, rows, chunk), BF16),
+            own, own, own, own, pltpu.VMEM((groups, TAPS), F32), double, double, own,
             toep, toep,
             pltpu.VMEM((2, groups, TAPS), F32),
             pltpu.VMEM((n_ctx, groups, TAPS), F32),
             pltpu.VMEM((n_quad, 8, TAPS), F32),
-            dma((4, n_chunks)), dma((3, n_chunks)),
+            dma((4, n_chunks)), dma,
             per_chunk, per_chunk, per_chunk, per_chunk, per_chunk, per_chunk,
             dma((n_ctx,)), dma((n_ctx,)), dma((n_quad,)), dma((n_quad,)),
         ],
         compiler_params=pltpu.CompilerParams(
             collective_id=0, has_side_effects=True, vmem_limit_bytes=48 << 20),
-    )(queries, key_feats, value_feats, cotangent, filters)
+    )(*[pltpu.with_memory_space_constraint(x, pltpu.HBM) for x in (queries, key_feats, value_feats, cotangent, filters)])
+    return pl.pallas_call(
+        write_back,
+        out_shape=out_shape,
+        in_specs=[pl.BlockSpec(memory_space=pl.ANY)] * 4,
+        out_specs=(hbm,) * 4,
+        scratch_shapes=[dma((4,))],
+        compiler_params=pltpu.CompilerParams(vmem_limit_bytes=16 << 20),
+    )(*results)
 
 
 def solution(mesh):

time: 38.2 us -> 31.5 us (0.82)
  local copies, waits for them, and re-layouts: 8.01 us -> 0 us
  Pallas kernels: 29.2 us -> 30.7 us
    unnamed x14 -> x0, local copies, waits for them, and re-layouts: 8.01 us -> none
    pallas_call x0 -> x1, Pallas kernels: none -> 1.18 us  [per_device(): pl.pallas_call(write_back, out_shape=out_shape, in_specs=[pl.BlockSpec(me...]
where the time goes in v2:
time: 31.5 us; the launch traced here: 31.4 us
  Pallas kernels  30.7 us (97%)
  between operations  0.64 us (2%)
    pallas_call x1, Pallas kernels, per_device(): pl.pallas_call(functools.partial(kernel, sizes, chunk, clip_level), out_s...  29.5 us
    pallas_call x1, Pallas kernels, per_device(): pl.pallas_call(write_back, out_shape=out_shape, in_specs=[pl.BlockSpec(me...  1.18 us

profile of v2, /device:TPU:1, one launch (start us, length us, event | category | flops | bytes accessed | tf_op | source)
XLA Modules:
  0.0 31.4 jit_solution(11272900280434914849)
XLA Ops:
  0.6 29.5 %shard_map.84 = (bf16[1,128,2048]{2,1,0:T(8,128)(2,1)S(1)}, bf16[1,128,2048]{2,1,0:T(8,128)(2,1)S(1)}, bf16[1,128,2048]{2,1,0:T(8,128)(2,1)S(1)}, f32[1,128,128]{2,1,0:T(8,128)S(1)}) custom-call(bf16[1,128,2048]{2,1,0:T(8,128)(2,1)} %q_hbm.1, bf16[1,128,2048]{2,1,0:T(8,128)(2,1)} %k_hbm.1, bf16[1,128,2048]{2,1,0:T(8,128)(2,1)} %v_hbm.1, ...), custom_call_target="tpu_custom_call" | custom-call | tf_op jit(solution)/shard_map/pallas_call | solution.py:315
  30.2 1.2 %shard_map.85 = (bf16[1,128,2048]{2,1,0:T(8,128)(2,1)}, bf16[1,128,2048]{2,1,0:T(8,128)(2,1)}, bf16[1,128,2048]{2,1,0:T(8,128)(2,1)}, f32[1,128,128]{2,1,0:T(8,128)}) custom-call(bf16[1,128,2048]{2,1,0:T(8,128)(2,1)S(1)} %get-tuple-element.8.refs_0_, bf16[1,128,2048]{2,1,0:T(8,128)(2,1)S(1)} %get-tuple-element.9.refs_1_, ...), custom_call_target="tpu_custom_call" | custom-call | tf_op jit(solution)/shard_map/pallas_call | solution.py:333

commit v3 on v2

--- a/solution.py
+++ b/solution.py
@@ -13,6 +13,7 @@
 LANES = 128
 PER = LANES // GROUP
 BLK = 32
+TBLK = 16
 WIDTH = 256
 MESH = pl.DeviceIdType.MESH
 F32 = jnp.float32
@@ -27,7 +28,7 @@
     sizes, chunk, clip_level,
     q_hbm, k_hbm, v_hbm, c_hbm, f_hbm,
     gq, gk, ho, gf_ref,
-    qv, kv, vv, cv, fv, wext, pext, dv, toep_b, toep_f, taps, raws, norms,
+    qv, kv, vv, cv, fv, wext, pext, dv, toep_b, toep_f, taps, raws, total, norms,
     in_sem, f_sem, w_send, w_recv, p_send, p_recv, d_send, d_recv,
     r_send, r_recv, n_send, n_recv,
 ):
@@ -144,6 +145,7 @@
         def _():
             send_p(i).start()
     each(n_chunks, elementwise)
+    each(groups // PER, lambda i: toeplitz(1, 1, toep_f, i))
 
     def lanes_of(i, s):
         return pl.ds(pl.multiple_of(i * chunk + s * LANES, LANES), LANES)
@@ -174,52 +176,55 @@
         @pl.when(pp > 0)
         def _():
             send_d(i).start()
-    each(n_chunks, backward)
 
     place = lax.broadcasted_iota(jnp.int32, (8, WIDTH), 0)
+
+    own_taps = owner[:TBLK]
 
     def tap_grad(i):
         for s in range(subs):
             cols = slice(s * LANES, (s + 1) * LANES)
             left, right = [], []
-            for a in range(blocks):
-                own = pext[i, rows + a * BLK : rows + (a + 1) * BLK, cols]
+            for a in range(rows // TBLK):
+                own = pext[i, rows + a * TBLK : rows + (a + 1) * TBLK, cols]
                 left.append(jnp.concatenate(
-                    [jnp.where(owner == g, own, jnp.zeros_like(own)) for g in range(PER)], axis=0))
-                right.append(wext[i, a * BLK : a * BLK + span, cols])
+                    [jnp.where(own_taps == g, own, jnp.zeros_like(own)) for g in range(PER)], axis=0))
+                right.append(wext[i, a * TBLK : a * TBLK + TBLK + TAPS, cols])
             pairs = dot(
                 jnp.concatenate(left, axis=1), jnp.concatenate(right, axis=1), ((1,), (1,)))
             pairs = jnp.concatenate(
-                [pairs, jnp.zeros((PER * BLK, WIDTH - span), F32)], axis=1)
+                [pairs, jnp.zeros((PER * TBLK, WIDTH - TBLK - TAPS), F32)], axis=1)
             sums = []
             for g in range(PER):
-                total = pairs[g * BLK : g * BLK + 8]
-                for b in range(8, BLK, 8):
-                    total = total + pltpu.roll(
-                        pairs[g * BLK + b : g * BLK + b + 8], WIDTH - b, 1)
+                partial = pairs[g * TBLK : g * TBLK + 8]
+                for b in range(8, TBLK, 8):
+                    partial = partial + pltpu.roll(
+                        pairs[g * TBLK + b : g * TBLK + b + 8], WIDTH - b, 1)
                 for bit in (1, 2, 4):
-                    moved = pltpu.roll(total, WIDTH - bit, 1)
-                    total = jnp.where((place & bit) != 0, moved, total)
-                sums.append(jnp.sum(total[:, :TAPS], axis=0, keepdims=True))
+                    moved = pltpu.roll(partial, WIDTH - bit, 1)
+                    partial = jnp.where((place & bit) != 0, moved, partial)
+                sums.append(jnp.sum(partial[:, :TAPS], axis=0, keepdims=True))
             at = pl.ds(pl.multiple_of((i * subs + s) * PER, PER), PER)
             raws[ctx, at, :] = jnp.concatenate(sums, axis=0)
-    each(n_chunks, tap_grad)
-
-    def send_r(d):
-        return pltpu.make_async_remote_copy(
-            src_ref=raws.at[ctx], dst_ref=raws.at[ctx],
-            send_sem=r_send.at[d], recv_sem=r_recv.at[d],
+
+    def share(d, slot, i):
+        part = raws.at[slot, pl.ds(pl.multiple_of(i * subs * PER, PER), subs * PER)]
+        return pltpu.make_async_remote_copy(
+            src_ref=part, dst_ref=part,
+            send_sem=r_send.at[d, i], recv_sem=r_recv.at[d, i],
             device_id=ctx_peer(d + 1), device_id_type=MESH)
 
-    def recv_r(d):
-        slot = lax.rem(ctx + n_ctx - 1 - d, n_ctx)
-        return pltpu.make_async_remote_copy(
-            src_ref=raws.at[slot], dst_ref=raws.at[slot],
-            send_sem=r_send.at[d], recv_sem=r_recv.at[d],
-            device_id=ctx_peer(d + 1), device_id_type=MESH)
-    each(n_ctx - 1, lambda d: send_r(d).start())
-
-    each(groups // PER, lambda i: toeplitz(1, 1, toep_f, i))
+    def send_r(d, i):
+        return share(d, ctx, i)
+
+    def recv_r(d, i):
+        return share(d, lax.rem(ctx + n_ctx - 1 - d, n_ctx), i)
+
+    def steps(i):
+        backward(i)
+        tap_grad(i)
+        each(n_ctx - 1, lambda d: send_r(d, i).start())
+    each(n_chunks, steps)
 
     def forward(i):
         @pl.when(has_prev)
@@ -232,12 +237,14 @@
                 mixed = filtered(toep_f, pext, i, s, a)
                 gq[0, here, lanes_of(i, s)] = (mixed * cv[i, here, cols].astype(F32)).astype(BF16)
 
-    each(n_chunks, forward)
-
-    each(n_ctx - 1, lambda d: recv_r(d).wait_recv())
+    early = n_chunks // 2
+    each(early, forward)
+
+    each(n_chunks, lambda i: each(n_ctx - 1, lambda d: recv_r(d, i).wait_recv()))
     summed = raws[0]
     for d in range(1, n_ctx):
         summed = summed + raws[d]
+    total[...] = summed
     squares = jnp.sum(summed * summed, axis=0, keepdims=True)
     norms[me] = jnp.broadcast_to(squares, (8, TAPS))
 
@@ -254,15 +261,16 @@
             send_sem=n_send.at[d], recv_sem=n_recv.at[d],
             device_id=quad(d + 1), device_id_type=MESH)
     each(n_quad - 1, lambda d: send_n(d).start())
+    each(n_chunks - early, lambda i: forward(early + i))
     each(n_quad - 1, lambda d: recv_n(d).wait_recv())
     squares = norms[0]
     for d in range(1, n_quad):
         squares = squares + norms[d]
     norm_sq = jnp.sum(squares[:1], axis=1, keepdims=True)
     factor = jnp.minimum(1.0, clip_level / (jnp.sqrt(norm_sq) + 1e-6))
-    gf_ref[0] = summed * factor
-
-    each(n_ctx - 1, lambda d: send_r(d).wait_send())
+    gf_ref[0] = total[...] * factor
+
+    each(n_chunks, lambda i: each(n_ctx - 1, lambda d: send_r(d, i).wait_send()))
     each(n_quad - 1, lambda d: send_n(d).wait_send())
 
     def drain(i):
@@ -322,10 +330,11 @@
             toep, toep,
             pltpu.VMEM((2, groups, TAPS), F32),
             pltpu.VMEM((n_ctx, groups, TAPS), F32),
+            pltpu.VMEM((groups, TAPS), F32),
             pltpu.VMEM((n_quad, 8, TAPS), F32),
             dma((4, n_chunks)), dma,
             per_chunk, per_chunk, per_chunk, per_chunk, per_chunk, per_chunk,
-            dma((n_ctx,)), dma((n_ctx,)), dma((n_quad,)), dma((n_quad,)),
+            dma((n_ctx, n_chunks)), dma((n_ctx, n_chunks)), dma((n_quad,)), dma((n_quad,)),
         ],
         compiler_params=pltpu.CompilerParams(
             collective_id=0, has_side_effects=True, vmem_limit_bytes=48 << 20),

time: 31.5 us -> 28.2 us (0.90)
  the two profiles are of different devices: /device:TPU:1 before, /device:TPU:0 now
where the time goes in v3:
time: 28.2 us; the launch traced here: 28 us
  Pallas kernels  27.4 us (97%)
  between operations  0.64 us (2%)
    pallas_call x1, Pallas kernels, per_device(): pl.pallas_call(functools.partial(kernel, sizes, chunk, clip_level), out_s...  26.2 us
    pallas_call x1, Pallas kernels, per_device(): pl.pallas_call(write_back, out_shape=out_shape, in_specs=[pl.BlockSpec(me...  1.18 us

profile of v3, /device:TPU:0, one launch (start us, length us, event | category | flops | bytes accessed | tf_op | source)
XLA Modules:
  0.0 28.0 jit_solution(11873968563603221386)
XLA Ops:
  0.6 26.2 %shard_map.84 = (bf16[1,128,2048]{2,1,0:T(8,128)(2,1)S(1)}, bf16[1,128,2048]{2,1,0:T(8,128)(2,1)S(1)}, bf16[1,128,2048]{2,1,0:T(8,128)(2,1)S(1)}, f32[1,128,128]{2,1,0:T(8,128)S(1)}) custom-call(bf16[1,128,2048]{2,1,0:T(8,128)(2,1)} %q_hbm.1, bf16[1,128,2048]{2,1,0:T(8,128)(2,1)} %k_hbm.1, bf16[1,128,2048]{2,1,0:T(8,128)(2,1)} %v_hbm.1, ...), custom_call_target="tpu_custom_call" | custom-call | tf_op jit(solution)/shard_map/pallas_call | solution.py:323
  26.8 1.2 %shard_map.85 = (bf16[1,128,2048]{2,1,0:T(8,128)(2,1)}, bf16[1,128,2048]{2,1,0:T(8,128)(2,1)}, bf16[1,128,2048]{2,1,0:T(8,128)(2,1)}, f32[1,128,128]{2,1,0:T(8,128)}) custom-call(bf16[1,128,2048]{2,1,0:T(8,128)(2,1)S(1)} %get-tuple-element.8.refs_0_, bf16[1,128,2048]{2,1,0:T(8,128)(2,1)S(1)} %get-tuple-element.9.refs_1_, ...), custom_call_target="tpu_custom_call" | custom-call | tf_op jit(solution)/shard_map/pallas_call | solution.py:342

commit v4 on v3

--- a/solution.py
+++ b/solution.py
@@ -12,7 +12,7 @@
 GROUP = 16
 LANES = 128
 PER = LANES // GROUP
-BLK = 32
+BLK = 16
 TBLK = 16
 WIDTH = 256
 MESH = pl.DeviceIdType.MESH
@@ -307,7 +307,7 @@
     n_ctx, n_tp, n_pp = sizes
     _, rows, channels = queries.shape
     groups = filters.shape[1]
-    chunk = math.gcd(channels, 256)
+    chunk = math.gcd(channels, 512)
     n_chunks = channels // chunk
     n_quad = n_tp * n_pp
     clip_level = 0.25 * math.sqrt(n_pp * n_tp * groups * TAPS)

time: 28.2 us -> 25.2 us (0.89)
  Pallas kernels: 27.4 us -> 24.4 us
    pallas_call x1, Pallas kernels: 26.2 us -> 23.2 us  [per_device(): pl.pallas_call(functools.partial(kernel, sizes, chunk, clip_level), out_s...]
where the time goes in v4:
time: 25.2 us; the launch traced here: 25 us
  Pallas kernels  24.4 us (97%)
  between operations  0.64 us (3%)
    pallas_call x1, Pallas kernels, per_device(): pl.pallas_call(functools.partial(kernel, sizes, chunk, clip_level), out_s...  23.2 us
    pallas_call x1, Pallas kernels, per_device(): pl.pallas_call(write_back, out_shape=out_shape, in_specs=[pl.BlockSpec(me...  1.18 us

profile of v4, /device:TPU:0, one launch (start us, length us, event | category | flops | bytes accessed | tf_op | source)
XLA Modules:
  0.0 25.0 jit_solution(15835842021013696438)
XLA Ops:
  0.6 23.2 %shard_map.84 = (bf16[1,128,2048]{2,1,0:T(8,128)(2,1)S(1)}, bf16[1,128,2048]{2,1,0:T(8,128)(2,1)S(1)}, bf16[1,128,2048]{2,1,0:T(8,128)(2,1)S(1)}, f32[1,128,128]{2,1,0:T(8,128)S(1)}) custom-call(bf16[1,128,2048]{2,1,0:T(8,128)(2,1)} %q_hbm.1, bf16[1,128,2048]{2,1,0:T(8,128)(2,1)} %k_hbm.1, bf16[1,128,2048]{2,1,0:T(8,128)(2,1)} %v_hbm.1, ...), custom_call_target="tpu_custom_call" | custom-call | tf_op jit(solution)/shard_map/pallas_call | solution.py:323
  23.9 1.2 %shard_map.85 = (bf16[1,128,2048]{2,1,0:T(8,128)(2,1)}, bf16[1,128,2048]{2,1,0:T(8,128)(2,1)}, bf16[1,128,2048]{2,1,0:T(8,128)(2,1)}, f32[1,128,128]{2,1,0:T(8,128)}) custom-call(bf16[1,128,2048]{2,1,0:T(8,128)(2,1)S(1)} %get-tuple-element.8.refs_0_, bf16[1,128,2048]{2,1,0:T(8,128)(2,1)S(1)} %get-tuple-element.9.refs_1_, ...), custom_call_target="tpu_custom_call" | custom-call | tf_op jit(solution)/shard_map/pallas_call | solution.py:342
